TPU v7x, 32 devices: a whole 2x2x4 slice. The times are simulated.
32 devices in a mesh: group: 2 (over y), pitch: 4 (over z), span: 2 (over x), radial: 2 (over core).
Axes of the slice: x: 2, y: 2, z: 4, core: 2. Of those that a mesh axis runs over, the one named last changes fastest.
Arguments:
- state: float32 [14, 6, 16, 8, 256], P('group', None, 'pitch', 'span', 'radial'), parts along dimension 0, may hold values from -0.5 to 2.8, as said below
- adjoint: float32 [14, 6, 16, 8, 256], P('group', None, 'pitch', 'span', 'radial'), parts along dimension 0, may hold values from -6 to 6
- displacement: float32 [6, 16, 8, 256], P('group', 'pitch', 'span', 'radial'), parts along dimension 0, may hold values from -0.1 to 0.1
Outputs:
- adjoint_residual: float32 [14, 6, 16, 8, 256], P('group', None, 'pitch', 'span', 'radial'), parts along dimension 0
- mesh_sensitivity: float32 [6, 16, 8, 256], P('group', 'pitch', 'span', 'radial'), parts along dimension 0
There are 2 independent parts, one for each index of `group`. A program takes and returns all parts, laid end to end along the dimension named above; each array names one. Nothing has to cross between parts.
Inputs may be any that keep to these rules, and one draw needn't show every extreme that they name: `state`: density within 0.8 to 1.2, momenta within -0.5 to 0.5, energy within 2.2 to 2.8, turbulence variable within 0.05 to 0.15.
All inputs are finite; a program needn't handle non-finite values.
Results may differ from a plain program's by a relative error of at most 0.0003.
Values sent between devices are 32-bit elements; how exact they have to be, the bound alone decides.
A program may use at most 64 MiB of HBM per device.

v0:
```python
import math

import jax
import jax.numpy as jnp
from jax import lax
from jax.experimental import pallas as pl
from jax.experimental.pallas import tpu as pltpu
from jax.sharding import PartitionSpec as P

NT = 7
NV = 6
LAMINAR_MU = 0.02
CV_CUBE = 7.1**3
SECOND_COEFF = 0.5
FOURTH_COEFF = 1.0 / 32.0
HEAT_DIFFUSIVE = 4.86
SIGMA_TURB = 2.0 / 3.0
PRODUCTION_COEF = 0.1355
CW_ONE = 3.24
FREQUENCY = 1.0
MESH = pl.DeviceIdType.MESH

CELLS = 16
ROWS = NV * CELLS
GROWS = NV * 8
PAD_STATE = (1.0, 0.0, 0.0, 0.0, 2.5, 0.1)


def coupling_matrix():
    out = [[0.0] * NT for _ in range(NT)]
    for n in range(NT):
        for m in range(NT):
            if n != m:
                out[n][m] = 0.5 * (-1.0) ** (n - m) / math.sin(math.pi * (n - m) / NT)
    return out


@jax.custom_jvp
def recip(x):
    return 1.0 / x


@recip.defjvp
def recip_jvp(primals, tangents):
    r = recip(primals[0])
    return r, -(r * r) * tangents[0]


@jax.custom_jvp
def root(x):
    return x * lax.rsqrt(x)


@root.defjvp
def root_jvp(primals, tangents):
    x = primals[0]
    y = lax.rsqrt(x)
    return x * y, (0.5 * y) * tangents[0]


def prim(u):
    inv = recip(u[0])
    vel = [u[1] * inv, u[2] * inv, u[3] * inv]
    kin = u[1] * vel[0] + u[2] * vel[1] + u[3] * vel[2]
    return inv, vel, 0.4 * (u[4] - 0.5 * kin)


def faces(d, cells, shift):
    n = len(cells)
    base = [prim(u) for u in cells]
    p = [b[2] for b in base]
    q = {}
    for i in range(1, n - 1):
        u = cells[i]
        inv, vel, pres = base[i]
        temp = pres * inv
        rn = u[0] * u[5]
        ratio = rn * (1.0 / LAMINAR_MU)
        cube = ratio * ratio * ratio
        visc = LAMINAR_MU + rn * (cube * recip(cube + CV_CUBE))
        un = vel[d]
        flux = [un * u[v] for v in range(NV)]
        flux[1 + d] = flux[1 + d] + pres
        flux[4] = flux[4] + pres * un
        radius = root(un * un + 0.01) + root(1.4 * temp)
        square = vel[0] * vel[0] + vel[1] * vel[1] + vel[2] * vel[2]
        ends = p[i + 1] + p[i - 1]
        ratio_p = (ends - 2.0 * pres) * recip(ends + 2.0 * pres)
        q[i] = (vel, temp, rn, visc, flux, radius, 0.5 * square + HEAT_DIFFUSIVE * temp, ratio_p * ratio_p)
    out = []
    for a in range(1, n - 2):
        b = a + 1
        qa, qb = q[a], q[b]
        eps_two = SECOND_COEFF * 0.5 * (qa[7] + qb[7])
        eps_four = FOURTH_COEFF * FOURTH_COEFF * recip(FOURTH_COEFF + eps_two)
        spread = 0.5 * (qa[5] + qb[5])
        two, four = spread * eps_two, spread * eps_four
        isp = recip(1.0 + shift[b] - shift[a])
        mu = 0.5 * (qa[3] + qb[3]) * isp
        turb = (LAMINAR_MU + 0.5 * (qa[2] + qb[2])) * (1.0 / SIGMA_TURB) * isp
        face = []
        for v in range(NV):
            jump = cells[b][v] - cells[a][v]
            third = cells[b + 1][v] - cells[a - 1][v] - 3.0 * jump
            f = 0.5 * (qa[4][v] + qb[4][v]) - two * jump + four * third
            if 1 <= v <= 3:
                f = f - mu * (qb[0][v - 1] - qa[0][v - 1])
            elif v == 4:
                f = f - mu * (qb[6] - qa[6])
            elif v == 5:
                f = f - turb * jump
            face.append(f)
        out.append(face)
    return out, q[1][4]


def source(pitch_up, pitch_dn, span_up, span_dn, rad_up, rad_dn, rho, nu, inv_wall):
    def gap(up, dn, k):
        return 0.5 * (up[k] * recip(up[0]) - dn[k] * recip(dn[0]))

    cx = gap(span_up, span_dn, 2) - gap(rad_up, rad_dn, 2)
    cy = gap(rad_up, rad_dn, 1) - gap(pitch_up, pitch_dn, 2)
    cz = gap(pitch_up, pitch_dn, 1) - gap(span_up, span_dn, 1)
    vort = root(cx * cx + cy * cy + cz * cz + 0.01)
    scaled = nu * inv_wall
    return rho * (CW_ONE * scaled * scaled - PRODUCTION_COEF * vort * nu)


def kernel(sizes, state, adjoint, disp, out_state, out_disp,
           own, lam, dis, other, other_lam, other_dis,
           pit_lo, pit_hi, spa_lo, spa_hi, dpit_lo, dpit_hi, dspa_lo, dspa_hi,
           send_lo, send_hi,
           upad, acc, gho, gacc, wbuf, dP, dS, dR, dG, cP, cS, cR, cG,
           rp_send_lo, rp_send_hi, rp_lo, rp_hi, rs_send_lo, rs_send_hi, rs_lo, rs_hi,
           rr_recv, rr_dsend, rr_drecv,
           local_sem, send_sem, recv_sem):
    n_pitch, n_span, n_rad, lanes = sizes
    ip = lax.axis_index("pitch")
    isp = lax.axis_index("span")
    ir = lax.axis_index("radial")
    ig = lax.axis_index("group")
    left = (ig, lax.rem(ip + n_pitch - 1, n_pitch), isp, ir)
    right = (ig, lax.rem(ip + 1, n_pitch), isp, ir)
    lower = (ig, ip, lax.rem(isp + n_span - 1, n_span), ir)
    upper = (ig, ip, lax.rem(isp + 1, n_span), ir)
    mate = (ig, ip, isp, 1 - ir)
    first = isp == 0
    last = isp == n_span - 1
    core0 = ir == 0

    loads = [
        pltpu.make_async_copy(adjoint, lam.at[pl.ds(0, NT * ROWS)], local_sem.at[1]),
        pltpu.make_async_copy(state, own.at[pl.ds(0, NT * ROWS)], local_sem.at[0]),
        pltpu.make_async_copy(disp, dis, local_sem.at[2]),
    ]
    for c in loads:
        c.start()

    bar = pltpu.get_barrier_semaphore()
    for who in (left, right, mate):
        pl.semaphore_signal(bar, inc=1, device_id=who, device_id_type=MESH)

    @pl.when(jnp.logical_not(first))
    def _():
        pl.semaphore_signal(bar, inc=1, device_id=lower, device_id_type=MESH)

    @pl.when(jnp.logical_not(last))
    def _():
        pl.semaphore_signal(bar, inc=1, device_id=upper, device_id_type=MESH)

    loads[1].wait()
    zero8 = jnp.zeros((8, lanes), jnp.float32)
    for v in range(NV):
        const = jnp.full((8, lanes), PAD_STATE[v], jnp.float32)
        for buf in (own, other):
            buf[pl.ds(NT * ROWS + v * CELLS, 8), :] = const
            buf[pl.ds(NT * ROWS + v * CELLS + 8, 8), :] = const
        for buf in (pit_lo, pit_hi, spa_lo, spa_hi):
            buf[pl.ds(NT * GROWS + v * 8, 8), :] = const
        for buf in (lam, other_lam):
            buf[pl.ds(NT * ROWS + v * CELLS, 8), :] = zero8
            buf[pl.ds(NT * ROWS + v * CELLS + 8, 8), :] = zero8

    def own_loop(p, c):
        for v in range(NV):
            for s in range(4):
                x = own[pl.ds(v * CELLS + p * 4 + s, 8, stride=ROWS), :]
                upad[v, p + 2, s + 2] = x
                buf = send_lo if s < 2 else send_hi
                buf[pl.ds(v * 8 + p * 2 + s % 2, 8, stride=GROWS), :] = x
        return c

    lax.fori_loop(0, 4, own_loop, 0)

    count = jnp.int32(3) + jnp.where(first, 0, 1) + jnp.where(last, 0, 1)
    pl.semaphore_wait(bar, count)

    def remote(k, src, dst, who):
        return pltpu.make_async_remote_copy(
            src_ref=src, dst_ref=dst, send_sem=send_sem.at[k], recv_sem=recv_sem.at[k],
            device_id=who, device_id_type=MESH)

    live = pl.ds(0, NT * GROWS)
    own3 = own
    c_rstate = remote(0, own.at[pl.ds(0, NT * ROWS)], other.at[pl.ds(0, NT * ROWS)], mate)
    c_rlam = remote(1, lam.at[pl.ds(0, NT * ROWS)], other_lam.at[pl.ds(0, NT * ROWS)], mate)
    c_rdis = remote(2, dis.at[pl.ds(32, 16)], other_dis, mate)
    st3 = state.reshape(NT * NV, CELLS, lanes)
    c_pup = remote(3, st3.at[:, pl.ds(8, 8), :], pit_lo.reshape(8 * NV, 8, lanes).at[pl.ds(0, NT * NV)], right)
    c_pdn = remote(4, st3.at[:, pl.ds(0, 8), :], pit_hi.reshape(8 * NV, 8, lanes).at[pl.ds(0, NT * NV)], left)
    c_dpup = remote(5, dis.at[pl.ds(8, 8)], dpit_lo, right)
    c_dpdn = remote(6, dis.at[pl.ds(0, 8)], dpit_hi, left)
    c_sup = remote(7, send_hi.at[live], spa_lo.at[live], upper)
    c_sdn = remote(8, send_lo.at[live], spa_hi.at[live], lower)
    c_dsup = remote(9, dis.at[pl.ds(16, 16)], dspa_lo, upper)
    c_dsdn = remote(10, dis.at[pl.ds(16, 16)], dspa_hi, lower)

    c_pup.start()
    c_pdn.start()
    c_rstate.start()
    loads[2].wait()
    c_dpup.start()
    c_dpdn.start()
    c_rdis.start()

    @pl.when(jnp.logical_not(first))
    def _():
        c_sdn.start()
        c_dsdn.start()

    @pl.when(jnp.logical_not(last))
    def _():
        c_sup.start()
        c_dsup.start()

    loads[0].wait()
    c_rlam.start()

    coup = coupling_matrix()

    def w_loop(j, c):
        base = pl.multiple_of(j * 8, 8)
        rows = [lam[pl.ds(n * ROWS + base, 8), :] for n in range(NT)]
        for m in range(NT):
            t = None
            for n in range(NT):
                if n != m:
                    x = coup[n][m] * rows[n]
                    t = x if t is None else t + x
            wbuf[pl.ds(m * ROWS + base, 8), :] = t
        wbuf[pl.ds(NT * ROWS + base, 8), :] = zero8
        return c

    lax.fori_loop(0, ROWS // 8, w_loop, 0)

    def z_loop(i, c):
        for v in range(NV):
            for j in range(8):
                acc[v, i, j] = zero8
        return c

    lax.fori_loop(0, 8, z_loop, 0)
    for k in range(24):
        cP[k] = zero8
        cS[k] = zero8

    lane = lax.broadcasted_iota(jnp.int32, (8, lanes), 1)
    lane0 = lane == 0
    lane_last = lane == lanes - 1
    low2 = lane < 2
    high2 = lane >= lanes - 2
    one = jnp.where(core0, lanes - 1, 1)
    three = jnp.where(core0, lanes - 3, 3)
    cell = jnp.where(core0, lane, lanes - 1 - lane)
    from_mate = cell >= lanes - 2
    ghost_mate = cell < 2
    ends = jnp.logical_or(lane0, lane_last)

    def ghost(x, y):
        return jnp.where(ghost_mate, y, jnp.where(ends, pltpu.roll(x, one, 1), pltpu.roll(x, three, 1)))

    def unghost(g):
        return jnp.where(cell == 0, pltpu.roll(g, lanes - one, 1),
                         jnp.where(cell == 1, pltpu.roll(g, lanes - three, 1), 0.0))

    def up1(x, g):
        return pltpu.roll(jnp.where(lane0, g, x), lanes - 1, 1)

    def up2(x, g):
        return pltpu.roll(jnp.where(low2, g, x), lanes - 2, 1)

    def dn1(x, g):
        return pltpu.roll(jnp.where(lane_last, g, x), 1, 1)

    def back(cm, c0, c1, c2):
        x, g = c0, None
        for c, amount, mask in ((cm, lanes - 1, lane_last), (c1, 1, lane0), (c2, 2, low2)):
            if c is None:
                continue
            z = pltpu.roll(c, amount, 1)
            part = jnp.where(mask, 0.0, z)
            gpart = jnp.where(mask, z, 0.0)
            x = part if x is None else x + part
            g = gpart if g is None else g + gpart
        return x, g

    def wide(ref, i):
        return jnp.broadcast_to(ref[pl.ds(i, 1), :], (8, lanes))

    def lam_at(i, v):
        return lam[pl.ds(v * CELLS + i, 8, stride=ROWS), :]

    c_rstate.wait_recv()
    c_rdis.wait_recv()
    c_rlam.wait_recv()

    def rad_loop(i, carry):
        p, s = i // 4, i % 4
        x = [upad[v, p + 2, s + 2] for v in range(NV)]
        g = [ghost(x[v], other[pl.ds(v * CELLS + i, 8, stride=ROWS), :]) for v in range(NV)]
        for v in range(NV):
            gho[v, i] = g[v]
        sh = wide(dis, 32 + i)
        shg = ghost(sh, wide(other_dis, i))
        dG[i] = shg
        cot, wallcot = [], []
        for v in range(NV):
            a = lam_at(i, v)
            y = other_lam[pl.ds(v * CELLS + i, 8, stride=ROWS), :]
            y = jnp.where(core0, y, 0.0)
            cot.append(a - up1(a, y))
            wallcot.append(jnp.where(jnp.logical_and(core0, lane0), -a, 0.0))
        cells = [[dn1(x[v], g[v]) for v in range(NV)], x,
                 [up1(x[v], g[v]) for v in range(NV)], [up2(x[v], g[v]) for v in range(NV)]]

        def f(cells, s1, s2):
            o, w = faces(2, cells, {1: s1, 2: s2})
            return o[0], w

        _, pull = jax.vjp(f, cells, sh, up1(sh, shg))
        bar_cells, b1, b2 = pull((cot, wallcot))
        for v in range(NV):
            xb, gb = back(bar_cells[0][v], bar_cells[1][v], bar_cells[2][v], bar_cells[3][v])
            acc[v, p + 2, s + 2] = xb
            gacc[v, i] = gb
        xb, gb = back(None, b1, b2, None)
        cR[i] = xb
        cG[i] = gb
        return carry

    lax.fori_loop(0, CELLS, rad_loop, 0)

    @pl.when(first)
    def _():
        def body(p, c):
            for v in range(NV):
                upad[v, p + 2, 1] = upad[v, p + 2, 2]
                upad[v, p + 2, 0] = upad[v, p + 2, 3]
            dS[pl.ds(p, 1), :] = dis[pl.ds(16 + p * 4, 1), :]
            return c
        lax.fori_loop(0, 4, body, 0)

    @pl.when(jnp.logical_not(first))
    def _():
        c_sup.wait_recv()
        c_dsup.wait_recv()

        def body(p, c):
            for v in range(NV):
                for s in range(2):
                    upad[v, p + 2, s] = spa_lo[pl.ds(v * 8 + p * 2 + s, 8, stride=GROWS), :]
            dS[pl.ds(p, 1), :] = dspa_lo[pl.ds(p * 4 + 3, 1), :]
            return c
        lax.fori_loop(0, 4, body, 0)

    @pl.when(last)
    def _():
        def body(p, c):
            for v in range(NV):
                upad[v, p + 2, 6] = upad[v, p + 2, 5]
                upad[v, p + 2, 7] = upad[v, p + 2, 4]
            dS[pl.ds(20 + p, 1), :] = dis[pl.ds(16 + p * 4 + 3, 1), :]
            return c
        lax.fori_loop(0, 4, body, 0)

    @pl.when(jnp.logical_not(last))
    def _():
        c_sdn.wait_recv()
        c_dsdn.wait_recv()

        def body(p, c):
            for v in range(NV):
                for s in range(2):
                    upad[v, p + 2, 6 + s] = spa_hi[pl.ds(v * 8 + p * 2 + s, 8, stride=GROWS), :]
            dS[pl.ds(20 + p, 1), :] = dspa_hi[pl.ds(p * 4, 1), :]
            return c
        lax.fori_loop(0, 4, body, 0)

    for k in range(4):
        for p in range(4):
            dS[pl.ds((k + 1) * 4 + p, 1), :] = dis[pl.ds(16 + p * 4 + k, 1), :]
            dP[pl.ds((k + 1) * 4 + p, 1), :] = dis[pl.ds(k * 4 + p, 1), :]

    def line(d, cells, shift, lams):
        cot = []
        for i in range(1, 6):
            row = []
            for v in range(NV):
                if i == 1:
                    row.append(-lams[0][v])
                elif i == 5:
                    row.append(lams[3][v])
                else:
                    row.append(lams[i - 2][v] - lams[i - 1][v])
            cot.append(row)
        _, pull = jax.vjp(lambda c, s: faces(d, c, dict(zip(range(1, 7), s)))[0], cells, shift)
        return pull(cot)

    def span_loop(p, carry):
        cells = [[upad[v, p + 2, k] for v in range(NV)] for k in range(8)]
        shift = [wide(dS, k * 4 + p) for k in range(6)]
        lams = [[lam_at(p * 4 + k, v) for v in range(NV)] for k in range(4)]
        bc, bs = line(1, cells, shift, lams)
        for k in range(8):
            for v in range(NV):
                acc[v, p + 2, k] += bc[k][v]
        for k in range(6):
            cS[k * 4 + p] += bs[k]
        return carry

    lax.fori_loop(0, 4, span_loop, 0)

    c_pup.wait_recv()
    c_dpup.wait_recv()
    c_pdn.wait_recv()
    c_dpdn.wait_recv()

    def pit_ghosts(s, c):
        for v in range(NV):
            for k in range(2):
                upad[v, k, s + 2] = pit_lo[pl.ds(v * 8 + k * 4 + s, 8, stride=GROWS), :]
                upad[v, 6 + k, s + 2] = pit_hi[pl.ds(v * 8 + k * 4 + s, 8, stride=GROWS), :]
        dP[pl.ds(s, 1), :] = dpit_lo[pl.ds(4 + s, 1), :]
        dP[pl.ds(20 + s, 1), :] = dpit_hi[pl.ds(s, 1), :]
        return c

    lax.fori_loop(0, 4, pit_ghosts, 0)

    def pitch_loop(s, carry):
        cells = [[upad[v, k, s + 2] for v in range(NV)] for k in range(8)]
        shift = [wide(dP, k * 4 + s) for k in range(6)]
        lams = [[lam_at(k * 4 + s, v) for v in range(NV)] for k in range(4)]
        bc, bs = line(0, cells, shift, lams)
        for k in range(8):
            for v in range(NV):
                acc[v, k, s + 2] += bc[k][v]
        for k in range(6):
            cP[k * 4 + s] += bs[k]
        return carry

    lax.fori_loop(0, 4, pitch_loop, 0)

    pos = (ir * lanes + lane).astype(jnp.float32) + 0.5
    inv_wall = 1.0 / jnp.minimum(pos, n_rad * lanes - pos)

    def cell_loop(i, carry):
        p, s = i // 4, i % 4
        a, b = p + 2, s + 2
        x = [upad[v, a, b] for v in range(NV)]
        g = [gho[v, i] for v in range(3)]
        pu = [upad[v, a + 1, b] for v in (0, 2, 3)]
        pd = [upad[v, a - 1, b] for v in (0, 2, 3)]
        su = [upad[v, a, b + 1] for v in (0, 1, 3)]
        sd = [upad[v, a, b - 1] for v in (0, 1, 3)]
        ru = [up1(x[v], g[v]) for v in (0, 1, 2)]
        rd = [dn1(x[v], g[v]) for v in (0, 1, 2)]
        _, pull = jax.vjp(lambda *t: source(*t, inv_wall), pu, pd, su, sd, ru, rd, x[0], x[5])
        bpu, bpd, bsu, bsd, bru, brd, brho, bnu = pull(lam_at(i, 5))
        for j, v in enumerate((0, 2, 3)):
            acc[v, a + 1, b] += bpu[j]
            acc[v, a - 1, b] += bpd[j]
        for j, v in enumerate((0, 1, 3)):
            acc[v, a, b + 1] += bsu[j]
            acc[v, a, b - 1] += bsd[j]
        extra = [brho, None, None, None, None, bnu]
        for j, v in enumerate((0, 1, 2)):
            xb, gb = back(brd[j], extra[v], bru[j], None)
            extra[v] = xb
            gacc[v, i] += gb
        dpu, dpd = wide(dP, (p + 2) * 4 + s), wide(dP, p * 4 + s)
        dsu, dsd = wide(dS, (s + 2) * 4 + p), wide(dS, s * 4 + p)
        sh, shg = wide(dis, 32 + i), dG[i]
        f0 = 1.0 + 0.5 * (dpu - dpd)
        f1 = 1.0 + 0.5 * (dsu - dsd)
        f2 = 1.0 + 0.5 * (up1(sh, shg) - dn1(sh, shg))
        f01 = f0 * f1
        vol = FREQUENCY * f01 * f2
        vbar = None
        for v in range(NV):
            w = wbuf[pl.ds(v * CELLS + i, 8, stride=ROWS), :]
            t = vol * w
            if extra[v] is not None:
                t = t + extra[v]
            acc[v, a, b] += t
            vbar = w * x[v] if vbar is None else vbar + w * x[v]
        h = (0.5 * FREQUENCY) * vbar
        h0 = h * (f1 * f2)
        h1 = h * (f0 * f2)
        h2 = h * f01
        cP[(p + 2) * 4 + s] += h0
        cP[p * 4 + s] -= h0
        cS[(s + 2) * 4 + p] += h1
        cS[s * 4 + p] -= h1
        xb, gb = back(-h2, None, h2, None)
        cR[i] += xb
        cG[i] += gb
        return carry

    lax.fori_loop(0, CELLS, cell_loop, 0)

    def total(x):
        return jnp.sum(x, axis=0, keepdims=True)

    gone = NT * GROWS + 8
    sent = pl.ds(0, gone)

    def pit_pack(s, c):
        for v in range(NV):
            for k in range(2):
                rp_send_lo[pl.ds(v * 8 + k * 4 + s, 8, stride=GROWS), :] = acc[v, k, s + 2]
                rp_send_hi[pl.ds(v * 8 + k * 4 + s, 8, stride=GROWS), :] = acc[v, 6 + k, s + 2]
        return c

    lax.fori_loop(0, 4, pit_pack, 0)
    for buf in (rp_send_lo, rp_send_hi):
        buf[pl.ds(NT * GROWS, 8), :] = zero8
    for s in range(4):
        rp_send_lo[pl.ds(NT * GROWS + s, 1), :] = total(cP[s])
        rp_send_hi[pl.ds(NT * GROWS + s, 1), :] = total(cP[20 + s])
    r_pup = remote(11, rp_send_hi.at[sent], rp_lo.at[sent], right)
    r_pdn = remote(12, rp_send_lo.at[sent], rp_hi.at[sent], left)
    r_pup.start()
    r_pdn.start()

    def spa_pack(p, c):
        for v in range(NV):
            for k in range(2):
                rs_send_lo[pl.ds(v * 8 + p * 2 + k, 8, stride=GROWS), :] = acc[v, p + 2, k]
                rs_send_hi[pl.ds(v * 8 + p * 2 + k, 8, stride=GROWS), :] = acc[v, p + 2, 6 + k]
        return c

    lax.fori_loop(0, 4, spa_pack, 0)
    for buf in (rs_send_lo, rs_send_hi):
        buf[pl.ds(NT * GROWS, 8), :] = zero8
    for p in range(4):
        rs_send_lo[pl.ds(NT * GROWS + p, 1), :] = total(cS[p])
        rs_send_hi[pl.ds(NT * GROWS + p, 1), :] = total(cS[20 + p])
    r_sup = remote(13, rs_send_hi.at[sent], rs_lo.at[sent], upper)
    r_sdn = remote(14, rs_send_lo.at[sent], rs_hi.at[sent], lower)

    @pl.when(jnp.logical_not(first))
    def _():
        r_sdn.start()

    @pl.when(jnp.logical_not(last))
    def _():
        r_sup.start()

    for i in range(CELLS):
        rr_dsend[pl.ds(i, 1), :] = total(cG[i])
    r_rad = remote(15, gacc, rr_recv, mate)
    r_rdis = remote(16, rr_dsend, rr_drecv, mate)
    r_rad.start()
    r_rdis.start()

    for p in range(4):
        for s in range(4):
            out_disp[pl.ds(p * 4 + s, 1), :] = total(cP[(p + 1) * 4 + s])
            out_disp[pl.ds(16 + p * 4 + s, 1), :] = total(cS[(s + 1) * 4 + p])
            out_disp[pl.ds(32 + p * 4 + s, 1), :] = total(cR[p * 4 + s] + unghost(cG[p * 4 + s]))

    @pl.when(first)
    def _():
        def body(p, c):
            for v in range(NV):
                acc[v, p + 2, 2] += acc[v, p + 2, 1]
                acc[v, p + 2, 3] += acc[v, p + 2, 0]
            out_disp[pl.ds(16 + p * 4, 1), :] += rs_send_lo[pl.ds(NT * GROWS + p, 1), :]
            return c
        lax.fori_loop(0, 4, body, 0)

    @pl.when(last)
    def _():
        def body(p, c):
            for v in range(NV):
                acc[v, p + 2, 5] += acc[v, p + 2, 6]
                acc[v, p + 2, 4] += acc[v, p + 2, 7]
            out_disp[pl.ds(16 + p * 4 + 3, 1), :] += rs_send_hi[pl.ds(NT * GROWS + p, 1), :]
            return c
        lax.fori_loop(0, 4, body, 0)

    r_rad.wait_recv()
    r_rdis.wait_recv()

    def rad_finish(i, c):
        p, s = i // 4, i % 4
        for v in range(NV):
            acc[v, p + 2, s + 2] += unghost(gacc[v, i]) + jnp.where(from_mate, rr_recv[v, i], 0.0)
        return c

    lax.fori_loop(0, CELLS, rad_finish, 0)
    for j in range(2):
        out_disp[pl.ds(32 + 8 * j, 8), :] += jnp.where(from_mate, rr_drecv[pl.ds(8 * j, 8), :], 0.0)

    @pl.when(jnp.logical_not(first))
    def _():
        r_sup.wait_recv()

        def body(p, c):
            for v in range(NV):
                for k in range(2):
                    acc[v, p + 2, 2 + k] += rs_lo[pl.ds(v * 8 + p * 2 + k, 8, stride=GROWS), :]
            out_disp[pl.ds(16 + p * 4, 1), :] += rs_lo[pl.ds(NT * GROWS + p, 1), :]
            return c
        lax.fori_loop(0, 4, body, 0)

    @pl.when(jnp.logical_not(last))
    def _():
        r_sdn.wait_recv()

        def body(p, c):
            for v in range(NV):
                for k in range(2):
                    acc[v, p + 2, 4 + k] += rs_hi[pl.ds(v * 8 + p * 2 + k, 8, stride=GROWS), :]
            out_disp[pl.ds(16 + p * 4 + 3, 1), :] += rs_hi[pl.ds(NT * GROWS + p, 1), :]
            return c
        lax.fori_loop(0, 4, body, 0)

    r_pup.wait_recv()
    r_pdn.wait_recv()

    def finish(s, c):
        for v in range(NV):
            for p in range(4):
                buf = rp_lo if p < 2 else rp_hi
                x = acc[v, p + 2, s + 2] + buf[pl.ds(v * 8 + (p % 2) * 4 + s, 8, stride=GROWS), :]
                out_state[pl.ds(v * CELLS + p * 4 + s, NT, stride=ROWS), :] = x[:NT]
        out_disp[pl.ds(s, 1), :] += rp_lo[pl.ds(NT * GROWS + s, 1), :]
        out_disp[pl.ds(12 + s, 1), :] += rp_hi[pl.ds(NT * GROWS + s, 1), :]
        return c

    lax.fori_loop(0, 4, finish, 0)

    for c in (c_rstate, c_rlam, c_rdis, c_pup, c_pdn, c_dpup, c_dpdn, r_pup, r_pdn, r_rad, r_rdis):
        c.wait_send()

    @pl.when(jnp.logical_not(first))
    def _():
        for c in (c_sdn, c_dsdn, r_sdn):
            c.wait_send()

    @pl.when(jnp.logical_not(last))
    def _():
        for c in (c_sup, c_dsup, r_sup):
            c.wait_send()


def solution(mesh):
    def body(state, adjoint, displacement):
        lanes = state.shape[-1]
        sizes = (mesh.shape["pitch"], mesh.shape["span"], mesh.shape["radial"], lanes)
        f32 = jnp.float32

        def vm(*lead):
            return pltpu.VMEM(tuple(lead) + (lanes,), f32)

        scratch = [
            vm(8 * ROWS), vm(8 * ROWS), vm(48), vm(8 * ROWS), vm(8 * ROWS), vm(16),
            vm(8 * GROWS), vm(8 * GROWS), vm(8 * GROWS), vm(8 * GROWS), vm(8), vm(8), vm(16), vm(16),
            vm(8 * GROWS), vm(8 * GROWS),
            vm(NV, 8, 8, 8), vm(NV, 8, 8, 8), vm(NV, CELLS, 8), vm(NV, CELLS, 8), vm(8 * ROWS),
            vm(24), vm(24), vm(16), vm(16, 8), vm(24, 8), vm(24, 8), vm(16, 8), vm(16, 8),
            vm(8 * GROWS), vm(8 * GROWS), vm(8 * GROWS), vm(8 * GROWS),
            vm(8 * GROWS), vm(8 * GROWS), vm(8 * GROWS), vm(8 * GROWS),
            vm(NV, CELLS, 8), vm(16), vm(16),
            pltpu.SemaphoreType.DMA((3,)), pltpu.SemaphoreType.DMA((17,)), pltpu.SemaphoreType.DMA((17,)),
        ]
        any_spec = pl.BlockSpec(memory_space=pl.ANY)
        vmem_spec = pl.BlockSpec(memory_space=pltpu.VMEM)
        out_state, out_disp = pl.pallas_call(
            lambda *refs: kernel(sizes, *refs),
            out_shape=(
                jax.ShapeDtypeStruct((NT * ROWS, lanes), f32),
                jax.ShapeDtypeStruct((3 * CELLS, lanes), f32),
            ),
            in_specs=[any_spec] * 3,
            out_specs=(vmem_spec, vmem_spec),
            scratch_shapes=scratch,
            compiler_params=pltpu.CompilerParams(
                collective_id=0, has_side_effects=True, vmem_limit_bytes=40 * 1024 * 1024),
            name="adjoint",
        )(
            state.reshape(NT * ROWS, lanes),
            adjoint.reshape(NT * ROWS, lanes),
            displacement.reshape(3 * CELLS, lanes),
        )
        return out_state.reshape(state.shape), out_disp.reshape(displacement.shape)

    spec = P("group", None, "pitch", "span", "radial")
    dspec = P("group", "pitch", "span", "radial")
    return jax.shard_map(
        body, mesh=mesh, in_specs=(spec, spec, dspec), out_specs=(spec, dspec), check_vma=False)
```

profile of v0, /device:TPU:0, one launch (start us, length us, event | category | flops | bytes accessed | tf_op | source)
XLA Modules:
  0.0 32.7 jit_solution(12615737386943987551)
XLA Ops:
  0.6 0.0 copy-start
  0.6 1.0 %copy-done = f32[7,6,4,4,128]{4,3,2,1,0:T(4,128)S(1)} copy-done((f32[7,6,4,4,128]{4,3,2,1,0:T(4,128)S(1)}, f32[7,6,4,4,128]{4,3,2,1,0:T(4,128)}, u32[]{:S(2)}) %copy-start) | copy-done | bytes 344088
  1.6 0.0 copy-start.1
  1.6 1.0 %copy-done.1 = f32[7,6,4,4,128]{4,3,2,1,0:T(4,128)S(1)} copy-done((f32[7,6,4,4,128]{4,3,2,1,0:T(4,128)S(1)}, f32[7,6,4,4,128]{4,3,2,1,0:T(4,128)}, u32[]{:S(2)}) %copy-start.1) | copy-done | bytes 344088
  2.6 0.0 copy-start.2
  2.6 0.7 %copy-done.2 = f32[3,4,4,128]{3,2,1,0:T(4,128)S(1)} copy-done((f32[3,4,4,128]{3,2,1,0:T(4,128)S(1)}, f32[3,4,4,128]{3,2,1,0:T(4,128)}, u32[]{:S(2)}) %copy-start.2) | copy-done | bytes 24600
  3.3 28.1 %adjoint.1 = (f32[672,128]{1,0:T(8,128)S(1)}, f32[48,128]{1,0:T(8,128)S(1)}) custom-call(f32[672,128]{1,0:T(8,128)S(1)} %bitcast.5, f32[672,128]{1,0:T(8,128)S(1)} %bitcast.6, f32[48,128]{1,0:T(8,128)S(1)} %bitcast.8), custom_call_target="tpu_custom_call" | custom-call | tf_op jit(solution)/shard_map/adjoint/pallas_call | solution.py:690
  31.4 0.7 %copy.7 = f32[7,6,4,4,128]{4,3,2,1,0:T(4,128)} copy(f32[7,6,4,4,128]{4,3,2,1,0:T(4,128)S(1)} %bitcast.7) | data formatting | bytes 688128
  32.1 0.6 %copy.8 = f32[3,4,4,128]{3,2,1,0:T(4,128)} copy(f32[3,4,4,128]{3,2,1,0:T(4,128)S(1)} %bitcast.9) | data formatting | bytes 49152
Async XLA Ops:
  0.6 1.0 %copy-start = (f32[7,6,4,4,128]{4,3,2,1,0:T(4,128)S(1)}, f32[7,6,4,4,128]{4,3,2,1,0:T(4,128)}, u32[]{:S(2)}) copy-start(f32[7,6,4,4,128]{4,3,2,1,0:T(4,128)} %param.3) | copy-start | bytes 1032196
  1.6 1.0 %copy-start.1 = (f32[7,6,4,4,128]{4,3,2,1,0:T(4,128)S(1)}, f32[7,6,4,4,128]{4,3,2,1,0:T(4,128)}, u32[]{:S(2)}) copy-start(f32[7,6,4,4,128]{4,3,2,1,0:T(4,128)} %param.4) | copy-start | bytes 1032196
  2.6 0.7 %copy-start.2 = (f32[3,4,4,128]{3,2,1,0:T(4,128)S(1)}, f32[3,4,4,128]{3,2,1,0:T(4,128)}, u32[]{:S(2)}) copy-start(f32[3,4,4,128]{3,2,1,0:T(4,128)} %param.5) | copy-start | bytes 73732
where the time goes:
time: 33 us; the launch traced here: 32.7 us
  Pallas kernels  28.1 us (85%)
  local copies, waits for them, and re-layouts  4.03 us (12%)
  between operations  0.65 us (2%)
    pallas_call x1, Pallas kernels, body(): pl.pallas_call(lambda *refs: kernel(sizes, *refs), out_shape=(jax.ShapeDt...  28.1 us
    unnamed x8, local copies, waits for them, and re-layouts  4.03 us

commit v1 on v0

--- a/solution.py
+++ b/solution.py
@@ -23,6 +23,7 @@
 CELLS = 16
 ROWS = NV * CELLS
 GROWS = NV * 8
+HROWS = NV * 4
 PAD_STATE = (1.0, 0.0, 0.0, 0.0, 2.5, 0.1)
 
 
@@ -129,7 +130,7 @@
 def kernel(sizes, state, adjoint, disp, out_state, out_disp,
            own, lam, dis, other, other_lam, other_dis,
            pit_lo, pit_hi, spa_lo, spa_hi, dpit_lo, dpit_hi, dspa_lo, dspa_hi,
-           send_lo, send_hi,
+           send_lo, send_hi, psend_lo, psend_hi,
            upad, acc, gho, gacc, wbuf, dP, dS, dR, dG, cP, cS, cR, cG,
            rp_send_lo, rp_send_hi, rp_lo, rp_hi, rs_send_lo, rs_send_hi, rs_lo, rs_hi,
            rr_recv, rr_dsend, rr_drecv,
@@ -175,22 +176,29 @@
         for buf in (own, other):
             buf[pl.ds(NT * ROWS + v * CELLS, 8), :] = const
             buf[pl.ds(NT * ROWS + v * CELLS + 8, 8), :] = const
-        for buf in (pit_lo, pit_hi, spa_lo, spa_hi):
+        for buf in (spa_lo, spa_hi):
             buf[pl.ds(NT * GROWS + v * 8, 8), :] = const
         for buf in (lam, other_lam):
             buf[pl.ds(NT * ROWS + v * CELLS, 8), :] = zero8
             buf[pl.ds(NT * ROWS + v * CELLS + 8, 8), :] = zero8
 
-    def own_loop(p, c):
-        for v in range(NV):
-            for s in range(4):
+    sub = lax.broadcasted_iota(jnp.int32, (8, lanes), 0)
+    for v in range(0, NV, 2):
+        const = jnp.where(sub < 4, PAD_STATE[v], PAD_STATE[v + 1])
+        for buf in (pit_lo, pit_hi):
+            for h in range(2):
+                buf[pl.ds(h * 8 * HROWS + NT * HROWS + v * 4, 8), :] = const
+
+    for p in range(4):
+        for s in range(4):
+            h, s2 = s // 2, s % 2
+            for v in range(NV):
                 x = own[pl.ds(v * CELLS + p * 4 + s, 8, stride=ROWS), :]
                 upad[v, p + 2, s + 2] = x
                 buf = send_lo if s < 2 else send_hi
-                buf[pl.ds(v * 8 + p * 2 + s % 2, 8, stride=GROWS), :] = x
-        return c
-
-    lax.fori_loop(0, 4, own_loop, 0)
+                buf[pl.ds(v * 8 + p * 2 + s2, 8, stride=GROWS), :] = x
+                buf = psend_lo if p < 2 else psend_hi
+                buf[pl.ds(h * 8 * HROWS + v * 4 + (p % 2) * 2 + s2, 8, stride=HROWS), :] = x
 
     count = jnp.int32(3) + jnp.where(first, 0, 1) + jnp.where(last, 0, 1)
     pl.semaphore_wait(bar, count)
@@ -201,13 +209,12 @@
             device_id=who, device_id_type=MESH)
 
     live = pl.ds(0, NT * GROWS)
-    own3 = own
     c_rstate = remote(0, own.at[pl.ds(0, NT * ROWS)], other.at[pl.ds(0, NT * ROWS)], mate)
     c_rlam = remote(1, lam.at[pl.ds(0, NT * ROWS)], other_lam.at[pl.ds(0, NT * ROWS)], mate)
     c_rdis = remote(2, dis.at[pl.ds(32, 16)], other_dis, mate)
-    st3 = state.reshape(NT * NV, CELLS, lanes)
-    c_pup = remote(3, st3.at[:, pl.ds(8, 8), :], pit_lo.reshape(8 * NV, 8, lanes).at[pl.ds(0, NT * NV)], right)
-    c_pdn = remote(4, st3.at[:, pl.ds(0, 8), :], pit_hi.reshape(8 * NV, 8, lanes).at[pl.ds(0, NT * NV)], left)
+    part = [pl.ds(h * 8 * HROWS, NT * HROWS) for h in range(2)]
+    c_pup = [remote((3, 17)[h], psend_hi.at[part[h]], pit_lo.at[part[h]], right) for h in range(2)]
+    c_pdn = [remote((4, 18)[h], psend_lo.at[part[h]], pit_hi.at[part[h]], left) for h in range(2)]
     c_dpup = remote(5, dis.at[pl.ds(8, 8)], dpit_lo, right)
     c_dpdn = remote(6, dis.at[pl.ds(0, 8)], dpit_hi, left)
     c_sup = remote(7, send_hi.at[live], spa_lo.at[live], upper)
@@ -215,12 +222,12 @@
     c_dsup = remote(9, dis.at[pl.ds(16, 16)], dspa_lo, upper)
     c_dsdn = remote(10, dis.at[pl.ds(16, 16)], dspa_hi, lower)
 
-    c_pup.start()
-    c_pdn.start()
-    c_rstate.start()
     loads[2].wait()
     c_dpup.start()
     c_dpdn.start()
+    c_pup[0].start()
+    c_pdn[0].start()
+    c_rstate.start()
     c_rdis.start()
 
     @pl.when(jnp.logical_not(first))
@@ -233,6 +240,8 @@
         c_sup.start()
         c_dsup.start()
 
+    c_pup[1].start()
+    c_pdn[1].start()
     loads[0].wait()
     c_rlam.start()
 
@@ -416,55 +425,11 @@
         _, pull = jax.vjp(lambda c, s: faces(d, c, dict(zip(range(1, 7), s)))[0], cells, shift)
         return pull(cot)
 
-    def span_loop(p, carry):
-        cells = [[upad[v, p + 2, k] for v in range(NV)] for k in range(8)]
-        shift = [wide(dS, k * 4 + p) for k in range(6)]
-        lams = [[lam_at(p * 4 + k, v) for v in range(NV)] for k in range(4)]
-        bc, bs = line(1, cells, shift, lams)
-        for k in range(8):
-            for v in range(NV):
-                acc[v, p + 2, k] += bc[k][v]
-        for k in range(6):
-            cS[k * 4 + p] += bs[k]
-        return carry
-
-    lax.fori_loop(0, 4, span_loop, 0)
-
-    c_pup.wait_recv()
-    c_dpup.wait_recv()
-    c_pdn.wait_recv()
-    c_dpdn.wait_recv()
-
-    def pit_ghosts(s, c):
-        for v in range(NV):
-            for k in range(2):
-                upad[v, k, s + 2] = pit_lo[pl.ds(v * 8 + k * 4 + s, 8, stride=GROWS), :]
-                upad[v, 6 + k, s + 2] = pit_hi[pl.ds(v * 8 + k * 4 + s, 8, stride=GROWS), :]
-        dP[pl.ds(s, 1), :] = dpit_lo[pl.ds(4 + s, 1), :]
-        dP[pl.ds(20 + s, 1), :] = dpit_hi[pl.ds(s, 1), :]
-        return c
-
-    lax.fori_loop(0, 4, pit_ghosts, 0)
-
-    def pitch_loop(s, carry):
-        cells = [[upad[v, k, s + 2] for v in range(NV)] for k in range(8)]
-        shift = [wide(dP, k * 4 + s) for k in range(6)]
-        lams = [[lam_at(k * 4 + s, v) for v in range(NV)] for k in range(4)]
-        bc, bs = line(0, cells, shift, lams)
-        for k in range(8):
-            for v in range(NV):
-                acc[v, k, s + 2] += bc[k][v]
-        for k in range(6):
-            cP[k * 4 + s] += bs[k]
-        return carry
-
-    lax.fori_loop(0, 4, pitch_loop, 0)
-
     pos = (ir * lanes + lane).astype(jnp.float32) + 0.5
     inv_wall = 1.0 / jnp.minimum(pos, n_rad * lanes - pos)
 
-    def cell_loop(i, carry):
-        p, s = i // 4, i % 4
+    def cell_work(p, s):
+        i = p * 4 + s
         a, b = p + 2, s + 2
         x = [upad[v, a, b] for v in range(NV)]
         g = [gho[v, i] for v in range(3)]
@@ -514,33 +479,89 @@
         xb, gb = back(-h2, None, h2, None)
         cR[i] += xb
         cG[i] += gb
-        return carry
-
-    lax.fori_loop(0, CELLS, cell_loop, 0)
+
+
+    def pitch_line(s):
+        cells = [[upad[v, k, s + 2] for v in range(NV)] for k in range(8)]
+        shift = [wide(dP, k * 4 + s) for k in range(6)]
+        lams = [[lam_at(k * 4 + s, v) for v in range(NV)] for k in range(4)]
+        bc, bs = line(0, cells, shift, lams)
+        for k in range(8):
+            for v in range(NV):
+                acc[v, k, s + 2] += bc[k][v]
+        for k in range(6):
+            cP[k * 4 + s] += bs[k]
 
     def total(x):
         return jnp.sum(x, axis=0, keepdims=True)
 
+    back_part = [pl.ds(h * 8 * HROWS, NT * HROWS + 8) for h in range(2)]
+    r_pup = [remote((11, 19)[h], rp_send_hi.at[back_part[h]], rp_lo.at[back_part[h]], right) for h in range(2)]
+    r_pdn = [remote((12, 20)[h], rp_send_lo.at[back_part[h]], rp_hi.at[back_part[h]], left) for h in range(2)]
+
+    def chunk(h):
+        c_pup[h].wait_recv()
+        c_pdn[h].wait_recv()
+        if h == 0:
+            c_dpup.wait_recv()
+            c_dpdn.wait_recv()
+            for s in range(4):
+                dP[pl.ds(s, 1), :] = dpit_lo[pl.ds(4 + s, 1), :]
+                dP[pl.ds(20 + s, 1), :] = dpit_hi[pl.ds(s, 1), :]
+
+        def ghosts(s2, c):
+            s = 2 * h + s2
+            for v in range(NV):
+                for k in range(2):
+                    row = pl.ds(h * 8 * HROWS + v * 4 + k * 2 + s2, 8, stride=HROWS)
+                    upad[v, k, s + 2] = pit_lo[row, :]
+                    upad[v, 6 + k, s + 2] = pit_hi[row, :]
+            pitch_line(s)
+            return c
+
+        lax.fori_loop(0, 2, ghosts, 0)
+
+        def cells_loop(j, c):
+            cell_work(j // 2, 2 * h + j % 2)
+            return c
+
+        lax.fori_loop(0, 8, cells_loop, 0)
+
+        for s2 in range(2):
+            s = 2 * h + s2
+            for v in range(NV):
+                for k in range(2):
+                    row = pl.ds(h * 8 * HROWS + v * 4 + k * 2 + s2, 8, stride=HROWS)
+                    rp_send_lo[row, :] = acc[v, k, s + 2]
+                    rp_send_hi[row, :] = acc[v, 6 + k, s + 2]
+        base = h * 8 * HROWS + NT * HROWS
+        for buf, k in ((rp_send_lo, 0), (rp_send_hi, 20)):
+            buf[pl.ds(base, 8), :] = zero8
+            for s2 in range(2):
+                buf[pl.ds(base + s2, 1), :] = total(cP[k + 2 * h + s2])
+        r_pup[h].start()
+        r_pdn[h].start()
+
+    chunk(0)
+
+    def span_loop(p, carry):
+        cells = [[upad[v, p + 2, k] for v in range(NV)] for k in range(8)]
+        shift = [wide(dS, k * 4 + p) for k in range(6)]
+        lams = [[lam_at(p * 4 + k, v) for v in range(NV)] for k in range(4)]
+        bc, bs = line(1, cells, shift, lams)
+        for k in range(8):
+            for v in range(NV):
+                acc[v, p + 2, k] += bc[k][v]
+        for k in range(6):
+            cS[k * 4 + p] += bs[k]
+        return carry
+
+    lax.fori_loop(0, 4, span_loop, 0)
+
+    chunk(1)
+
     gone = NT * GROWS + 8
     sent = pl.ds(0, gone)
-
-    def pit_pack(s, c):
-        for v in range(NV):
-            for k in range(2):
-                rp_send_lo[pl.ds(v * 8 + k * 4 + s, 8, stride=GROWS), :] = acc[v, k, s + 2]
-                rp_send_hi[pl.ds(v * 8 + k * 4 + s, 8, stride=GROWS), :] = acc[v, 6 + k, s + 2]
-        return c
-
-    lax.fori_loop(0, 4, pit_pack, 0)
-    for buf in (rp_send_lo, rp_send_hi):
-        buf[pl.ds(NT * GROWS, 8), :] = zero8
-    for s in range(4):
-        rp_send_lo[pl.ds(NT * GROWS + s, 1), :] = total(cP[s])
-        rp_send_hi[pl.ds(NT * GROWS + s, 1), :] = total(cP[20 + s])
-    r_pup = remote(11, rp_send_hi.at[sent], rp_lo.at[sent], right)
-    r_pdn = remote(12, rp_send_lo.at[sent], rp_hi.at[sent], left)
-    r_pup.start()
-    r_pdn.start()
 
     def spa_pack(p, c):
         for v in range(NV):
@@ -636,22 +657,22 @@
             return c
         lax.fori_loop(0, 4, body, 0)
 
-    r_pup.wait_recv()
-    r_pdn.wait_recv()
-
-    def finish(s, c):
-        for v in range(NV):
-            for p in range(4):
-                buf = rp_lo if p < 2 else rp_hi
-                x = acc[v, p + 2, s + 2] + buf[pl.ds(v * 8 + (p % 2) * 4 + s, 8, stride=GROWS), :]
-                out_state[pl.ds(v * CELLS + p * 4 + s, NT, stride=ROWS), :] = x[:NT]
-        out_disp[pl.ds(s, 1), :] += rp_lo[pl.ds(NT * GROWS + s, 1), :]
-        out_disp[pl.ds(12 + s, 1), :] += rp_hi[pl.ds(NT * GROWS + s, 1), :]
-        return c
-
-    lax.fori_loop(0, 4, finish, 0)
-
-    for c in (c_rstate, c_rlam, c_rdis, c_pup, c_pdn, c_dpup, c_dpdn, r_pup, r_pdn, r_rad, r_rdis):
+    for h in range(2):
+        r_pup[h].wait_recv()
+        r_pdn[h].wait_recv()
+        for s2 in range(2):
+            s = 2 * h + s2
+            for v in range(NV):
+                for p in range(4):
+                    buf = rp_lo if p < 2 else rp_hi
+                    row = pl.ds(h * 8 * HROWS + v * 4 + (p % 2) * 2 + s2, 8, stride=HROWS)
+                    x = acc[v, p + 2, s + 2] + buf[row, :]
+                    out_state[pl.ds(v * CELLS + p * 4 + s, NT, stride=ROWS), :] = x[:NT]
+            row = pl.ds(h * 8 * HROWS + NT * HROWS + s2, 1)
+            out_disp[pl.ds(s, 1), :] += rp_lo[row, :]
+            out_disp[pl.ds(12 + s, 1), :] += rp_hi[row, :]
+
+    for c in (c_rstate, c_rlam, c_rdis, *c_pup, *c_pdn, c_dpup, c_dpdn, *r_pup, *r_pdn, r_rad, r_rdis):
         c.wait_send()
 
     @pl.when(jnp.logical_not(first))
@@ -677,13 +698,13 @@
         scratch = [
             vm(8 * ROWS), vm(8 * ROWS), vm(48), vm(8 * ROWS), vm(8 * ROWS), vm(16),
             vm(8 * GROWS), vm(8 * GROWS), vm(8 * GROWS), vm(8 * GROWS), vm(8), vm(8), vm(16), vm(16),
-            vm(8 * GROWS), vm(8 * GROWS),
+            vm(8 * GROWS), vm(8 * GROWS), vm(8 * GROWS), vm(8 * GROWS),
             vm(NV, 8, 8, 8), vm(NV, 8, 8, 8), vm(NV, CELLS, 8), vm(NV, CELLS, 8), vm(8 * ROWS),
             vm(24), vm(24), vm(16), vm(16, 8), vm(24, 8), vm(24, 8), vm(16, 8), vm(16, 8),
             vm(8 * GROWS), vm(8 * GROWS), vm(8 * GROWS), vm(8 * GROWS),
             vm(8 * GROWS), vm(8 * GROWS), vm(8 * GROWS), vm(8 * GROWS),
             vm(NV, CELLS, 8), vm(16), vm(16),
-            pltpu.SemaphoreType.DMA((3,)), pltpu.SemaphoreType.DMA((17,)), pltpu.SemaphoreType.DMA((17,)),
+            pltpu.SemaphoreType.DMA((3,)), pltpu.SemaphoreType.DMA((21,)), pltpu.SemaphoreType.DMA((21,)),
         ]
         any_spec = pl.BlockSpec(memory_space=pl.ANY)
         vmem_spec = pl.BlockSpec(memory_space=pltpu.VMEM)
@@ -697,7 +718,7 @@
             out_specs=(vmem_spec, vmem_spec),
             scratch_shapes=scratch,
             compiler_params=pltpu.CompilerParams(
-                collective_id=0, has_side_effects=True, vmem_limit_bytes=40 * 1024 * 1024),
+                collective_id=0, has_side_effects=True, vmem_limit_bytes=60 * 1024 * 1024),
             name="adjoint",
         )(
             state.reshape(NT * ROWS, lanes),

time: 33 us -> 28.7 us (0.87)
  Pallas kernels: 28.1 us -> 25.6 us
  local copies, waits for them, and re-layouts: 4.03 us -> 2.35 us
    pallas_call x1, Pallas kernels: 28.1 us -> 25.6 us  [body(): pl.pallas_call(lambda *refs: kernel(sizes, *refs), out_shape=(jax.ShapeDt...]
    unnamed x8 -> x4, local copies, waits for them, and re-layouts: 4.03 us -> 2.35 us
where the time goes in v1:
time: 28.7 us; the launch traced here: 28.6 us
  Pallas kernels  25.6 us (89%)
  local copies, waits for them, and re-layouts  2.35 us (8%)
  between operations  0.65 us (2%)
    pallas_call x1, Pallas kernels, body(): pl.pallas_call(lambda *refs: kernel(sizes, *refs), out_shape=(jax.ShapeDt...  25.6 us
    unnamed x4, local copies, waits for them, and re-layouts  2.35 us

profile of v1, /device:TPU:0, one launch (start us, length us, event | category | flops | bytes accessed | tf_op | source)
XLA Modules:
  0.0 28.6 jit_solution(6580549447694068300)
XLA Ops:
  0.6 25.6 %adjoint.1 = (f32[672,128]{1,0:T(8,128)}, f32[48,128]{1,0:T(8,128)}) custom-call(f32[672,128]{1,0:T(8,128)} %bitcast.5, f32[672,128]{1,0:T(8,128)} %bitcast.6, f32[48,128]{1,0:T(8,128)} %bitcast.8), custom_call_target="tpu_custom_call" | custom-call | tf_op jit(solution)/shard_map/adjoint/pallas_call | solution.py:711
  26.2 0.0 copy-start
  26.2 1.7 %copy.7 = f32[7,6,4,4,128]{4,3,2,1,0:T(4,128)} copy(f32[7,6,4,4,128]{4,3,2,1,0:T(4,128)} %bitcast.7) | data formatting | bytes 688128
  27.9 0.0 copy-done
  27.9 0.6 %copy.8 = f32[3,4,4,128]{3,2,1,0:T(4,128)} copy(f32[3,4,4,128]{3,2,1,0:T(4,128)S(1)} %bitcast.9) | data formatting | bytes 49152
Async XLA Ops:
  26.2 1.7 %copy-start = (f32[48,128]{1,0:T(8,128)S(1)}, f32[48,128]{1,0:T(8,128)}, u32[]{:S(2)}) copy-start(f32[48,128]{1,0:T(8,128)} %get-tuple-element.5) | copy-start | bytes 73732

commit v2 on v1

--- a/solution.py
+++ b/solution.py
@@ -24,6 +24,7 @@
 ROWS = NV * CELLS
 GROWS = NV * 8
 HROWS = NV * 4
+QROWS = NV * 2
 PAD_STATE = (1.0, 0.0, 0.0, 0.0, 2.5, 0.1)
 
 
@@ -130,7 +131,7 @@
 def kernel(sizes, state, adjoint, disp, out_state, out_disp,
            own, lam, dis, other, other_lam, other_dis,
            pit_lo, pit_hi, spa_lo, spa_hi, dpit_lo, dpit_hi, dspa_lo, dspa_hi,
-           send_lo, send_hi, psend_lo, psend_hi,
+           send_lo, send_hi, psend_lo, psend_hi, lsend, lrecv,
            upad, acc, gho, gacc, wbuf, dP, dS, dR, dG, cP, cS, cR, cG,
            rp_send_lo, rp_send_hi, rp_lo, rp_hi, rs_send_lo, rs_send_hi, rs_lo, rs_hi,
            rr_recv, rr_dsend, rr_drecv,
@@ -150,8 +151,8 @@
     core0 = ir == 0
 
     loads = [
+        pltpu.make_async_copy(state, own.at[pl.ds(0, NT * ROWS)], local_sem.at[0]),
         pltpu.make_async_copy(adjoint, lam.at[pl.ds(0, NT * ROWS)], local_sem.at[1]),
-        pltpu.make_async_copy(state, own.at[pl.ds(0, NT * ROWS)], local_sem.at[0]),
         pltpu.make_async_copy(disp, dis, local_sem.at[2]),
     ]
     for c in loads:
@@ -169,7 +170,6 @@
     def _():
         pl.semaphore_signal(bar, inc=1, device_id=upper, device_id_type=MESH)
 
-    loads[1].wait()
     zero8 = jnp.zeros((8, lanes), jnp.float32)
     for v in range(NV):
         const = jnp.full((8, lanes), PAD_STATE[v], jnp.float32)
@@ -185,9 +185,14 @@
     sub = lax.broadcasted_iota(jnp.int32, (8, lanes), 0)
     for v in range(0, NV, 2):
         const = jnp.where(sub < 4, PAD_STATE[v], PAD_STATE[v + 1])
-        for buf in (pit_lo, pit_hi):
-            for h in range(2):
-                buf[pl.ds(h * 8 * HROWS + NT * HROWS + v * 4, 8), :] = const
+        for h in range(2):
+            pit_hi[pl.ds(h * 8 * HROWS + NT * HROWS + v * 4, 8), :] = const
+    const = jnp.where(sub < 4, jnp.where(sub < 2, PAD_STATE[2], PAD_STATE[3]),
+                      jnp.where(sub < 6, PAD_STATE[4], PAD_STATE[5]))
+    for h in range(2):
+        pit_lo[pl.ds(h * 8 * QROWS + NT * QROWS + 4, 8), :] = const
+        lrecv[pl.ds(h * 8 * QROWS + NT * QROWS + 4, 8), :] = zero8
+    loads[0].wait()
 
     for p in range(4):
         for s in range(4):
@@ -197,8 +202,16 @@
                 upad[v, p + 2, s + 2] = x
                 buf = send_lo if s < 2 else send_hi
                 buf[pl.ds(v * 8 + p * 2 + s2, 8, stride=GROWS), :] = x
-                buf = psend_lo if p < 2 else psend_hi
-                buf[pl.ds(h * 8 * HROWS + v * 4 + (p % 2) * 2 + s2, 8, stride=HROWS), :] = x
+                if p < 2:
+                    psend_lo[pl.ds(h * 8 * HROWS + v * 4 + p * 2 + s2, 8, stride=HROWS), :] = x
+                if p == 3:
+                    psend_hi[pl.ds(h * 8 * QROWS + v * 2 + s2, 8, stride=QROWS), :] = x
+
+    loads[1].wait()
+    for s in range(4):
+        for v in range(NV):
+            lsend[pl.ds((s // 2) * 8 * QROWS + v * 2 + s % 2, 8, stride=QROWS), :] = (
+                lam[pl.ds(v * CELLS + s, 8, stride=ROWS), :])
 
     count = jnp.int32(3) + jnp.where(first, 0, 1) + jnp.where(last, 0, 1)
     pl.semaphore_wait(bar, count)
@@ -213,7 +226,9 @@
     c_rlam = remote(1, lam.at[pl.ds(0, NT * ROWS)], other_lam.at[pl.ds(0, NT * ROWS)], mate)
     c_rdis = remote(2, dis.at[pl.ds(32, 16)], other_dis, mate)
     part = [pl.ds(h * 8 * HROWS, NT * HROWS) for h in range(2)]
-    c_pup = [remote((3, 17)[h], psend_hi.at[part[h]], pit_lo.at[part[h]], right) for h in range(2)]
+    one_layer = [pl.ds(h * 8 * QROWS, NT * QROWS + 4) for h in range(2)]
+    c_pup = [remote((3, 17)[h], psend_hi.at[one_layer[h]], pit_lo.at[one_layer[h]], right) for h in range(2)]
+    c_lam = [remote((21, 22)[h], lsend.at[one_layer[h]], lrecv.at[one_layer[h]], left) for h in range(2)]
     c_pdn = [remote((4, 18)[h], psend_lo.at[part[h]], pit_hi.at[part[h]], left) for h in range(2)]
     c_dpup = remote(5, dis.at[pl.ds(8, 8)], dpit_lo, right)
     c_dpdn = remote(6, dis.at[pl.ds(0, 8)], dpit_hi, left)
@@ -227,6 +242,7 @@
     c_dpdn.start()
     c_pup[0].start()
     c_pdn[0].start()
+    c_lam[0].start()
     c_rstate.start()
     c_rdis.start()
 
@@ -242,7 +258,7 @@
 
     c_pup[1].start()
     c_pdn[1].start()
-    loads[0].wait()
+    c_lam[1].start()
     c_rlam.start()
 
     coup = coupling_matrix()
@@ -441,17 +457,12 @@
         rd = [dn1(x[v], g[v]) for v in (0, 1, 2)]
         _, pull = jax.vjp(lambda *t: source(*t, inv_wall), pu, pd, su, sd, ru, rd, x[0], x[5])
         bpu, bpd, bsu, bsd, bru, brd, brho, bnu = pull(lam_at(i, 5))
-        for j, v in enumerate((0, 2, 3)):
-            acc[v, a + 1, b] += bpu[j]
-            acc[v, a - 1, b] += bpd[j]
-        for j, v in enumerate((0, 1, 3)):
-            acc[v, a, b + 1] += bsu[j]
-            acc[v, a, b - 1] += bsd[j]
+        ghosts_to, terms = [], []
         extra = [brho, None, None, None, None, bnu]
         for j, v in enumerate((0, 1, 2)):
             xb, gb = back(brd[j], extra[v], bru[j], None)
             extra[v] = xb
-            gacc[v, i] += gb
+            ghosts_to.append(gb)
         dpu, dpd = wide(dP, (p + 2) * 4 + s), wide(dP, p * 4 + s)
         dsu, dsd = wide(dS, (s + 2) * 4 + p), wide(dS, s * 4 + p)
         sh, shg = wide(dis, 32 + i), dG[i]
@@ -466,42 +477,59 @@
             t = vol * w
             if extra[v] is not None:
                 t = t + extra[v]
-            acc[v, a, b] += t
+            terms.append(t)
             vbar = w * x[v] if vbar is None else vbar + w * x[v]
         h = (0.5 * FREQUENCY) * vbar
         h0 = h * (f1 * f2)
         h1 = h * (f0 * f2)
         h2 = h * f01
-        cP[(p + 2) * 4 + s] += h0
-        cP[p * 4 + s] -= h0
-        cS[(s + 2) * 4 + p] += h1
-        cS[s * 4 + p] -= h1
         xb, gb = back(-h2, None, h2, None)
-        cR[i] += xb
-        cG[i] += gb
-
-
-    def pitch_line(s):
-        cells = [[upad[v, k, s + 2] for v in range(NV)] for k in range(8)]
-        shift = [wide(dP, k * 4 + s) for k in range(6)]
+
+        def add():
+            for j, v in enumerate((0, 2, 3)):
+                acc[v, a + 1, b] += bpu[j]
+                acc[v, a - 1, b] += bpd[j]
+            for j, v in enumerate((0, 1, 3)):
+                acc[v, a, b + 1] += bsu[j]
+                acc[v, a, b - 1] += bsd[j]
+            for v in range(3):
+                gacc[v, i] += ghosts_to[v]
+            for v in range(NV):
+                acc[v, a, b] += terms[v]
+            cP[(p + 2) * 4 + s] += h0
+            cP[p * 4 + s] -= h0
+            cS[(s + 2) * 4 + p] += h1
+            cS[s * 4 + p] -= h1
+            cR[i] += xb
+            cG[i] += gb
+
+        return add
+
+    def pitch_line(s, h, s2):
+        cells = [[upad[v, k, s + 2] for v in range(NV)] for k in range(1, 8)]
+        shift = [wide(dP, k * 4 + s) for k in range(1, 6)]
         lams = [[lam_at(k * 4 + s, v) for v in range(NV)] for k in range(4)]
-        bc, bs = line(0, cells, shift, lams)
-        for k in range(8):
-            for v in range(NV):
-                acc[v, k, s + 2] += bc[k][v]
-        for k in range(6):
-            cP[k * 4 + s] += bs[k]
+        lams.append([lrecv[pl.ds(h * 8 * QROWS + v * 2 + s2, 8, stride=QROWS), :] for v in range(NV)])
+        cot = [[lams[k][v] - lams[k + 1][v] for v in range(NV)] for k in range(4)]
+        _, pull = jax.vjp(lambda c, t: faces(0, c, dict(zip(range(1, 6), t)))[0], cells, shift)
+        bc, bs = pull(cot)
+        for k in range(7):
+            for v in range(NV):
+                acc[v, k + 1, s + 2] += bc[k][v]
+        for k in range(5):
+            cP[(k + 1) * 4 + s] += bs[k]
 
     def total(x):
         return jnp.sum(x, axis=0, keepdims=True)
 
     back_part = [pl.ds(h * 8 * HROWS, NT * HROWS + 8) for h in range(2)]
     r_pup = [remote((11, 19)[h], rp_send_hi.at[back_part[h]], rp_lo.at[back_part[h]], right) for h in range(2)]
-    r_pdn = [remote((12, 20)[h], rp_send_lo.at[back_part[h]], rp_hi.at[back_part[h]], left) for h in range(2)]
+    r_pdn = [remote((12, 20)[h], rp_send_lo.at[one_layer[h]], rp_hi.at[one_layer[h]], left) for h in range(2)]
 
     def chunk(h):
         c_pup[h].wait_recv()
         c_pdn[h].wait_recv()
+        c_lam[h].wait_recv()
         if h == 0:
             c_dpup.wait_recv()
             c_dpdn.wait_recv()
@@ -512,33 +540,34 @@
         def ghosts(s2, c):
             s = 2 * h + s2
             for v in range(NV):
+                upad[v, 1, s + 2] = pit_lo[pl.ds(h * 8 * QROWS + v * 2 + s2, 8, stride=QROWS), :]
                 for k in range(2):
                     row = pl.ds(h * 8 * HROWS + v * 4 + k * 2 + s2, 8, stride=HROWS)
-                    upad[v, k, s + 2] = pit_lo[row, :]
                     upad[v, 6 + k, s + 2] = pit_hi[row, :]
-            pitch_line(s)
+            pitch_line(s, h, s2)
             return c
 
         lax.fori_loop(0, 2, ghosts, 0)
 
-        def cells_loop(j, c):
-            cell_work(j // 2, 2 * h + j % 2)
-            return c
-
-        lax.fori_loop(0, 8, cells_loop, 0)
-
+        def cells_loop(p, c):
+            adds = [cell_work(p, 2 * h), cell_work(p, 2 * h + 1)]
+            for add in adds:
+                add()
+            return c
+
+        lax.fori_loop(0, 4, cells_loop, 0)
+
+        base = h * 8 * HROWS
+        low = h * 8 * QROWS
         for s2 in range(2):
             s = 2 * h + s2
             for v in range(NV):
+                rp_send_lo[pl.ds(low + v * 2 + s2, 8, stride=QROWS), :] = acc[v, 1, s + 2]
                 for k in range(2):
-                    row = pl.ds(h * 8 * HROWS + v * 4 + k * 2 + s2, 8, stride=HROWS)
-                    rp_send_lo[row, :] = acc[v, k, s + 2]
-                    rp_send_hi[row, :] = acc[v, 6 + k, s + 2]
-        base = h * 8 * HROWS + NT * HROWS
-        for buf, k in ((rp_send_lo, 0), (rp_send_hi, 20)):
-            buf[pl.ds(base, 8), :] = zero8
-            for s2 in range(2):
-                buf[pl.ds(base + s2, 1), :] = total(cP[k + 2 * h + s2])
+                    rp_send_hi[pl.ds(base + v * 4 + k * 2 + s2, 8, stride=HROWS), :] = acc[v, 6 + k, s + 2]
+        for s2 in range(2):
+            rp_send_lo[pl.ds(low + NT * QROWS + s2, 1), :] = total(cP[2 * h + s2])
+            rp_send_hi[pl.ds(base + NT * HROWS + s2, 1), :] = total(cP[20 + 2 * h + s2])
         r_pup[h].start()
         r_pdn[h].start()
 
@@ -664,15 +693,16 @@
             s = 2 * h + s2
             for v in range(NV):
                 for p in range(4):
-                    buf = rp_lo if p < 2 else rp_hi
-                    row = pl.ds(h * 8 * HROWS + v * 4 + (p % 2) * 2 + s2, 8, stride=HROWS)
-                    x = acc[v, p + 2, s + 2] + buf[row, :]
+                    x = acc[v, p + 2, s + 2]
+                    if p < 2:
+                        x = x + rp_lo[pl.ds(h * 8 * HROWS + v * 4 + p * 2 + s2, 8, stride=HROWS), :]
+                    if p == 3:
+                        x = x + rp_hi[pl.ds(h * 8 * QROWS + v * 2 + s2, 8, stride=QROWS), :]
                     out_state[pl.ds(v * CELLS + p * 4 + s, NT, stride=ROWS), :] = x[:NT]
-            row = pl.ds(h * 8 * HROWS + NT * HROWS + s2, 1)
-            out_disp[pl.ds(s, 1), :] += rp_lo[row, :]
-            out_disp[pl.ds(12 + s, 1), :] += rp_hi[row, :]
-
-    for c in (c_rstate, c_rlam, c_rdis, *c_pup, *c_pdn, c_dpup, c_dpdn, *r_pup, *r_pdn, r_rad, r_rdis):
+            out_disp[pl.ds(s, 1), :] += rp_lo[pl.ds(h * 8 * HROWS + NT * HROWS + s2, 1), :]
+            out_disp[pl.ds(12 + s, 1), :] += rp_hi[pl.ds(h * 8 * QROWS + NT * QROWS + s2, 1), :]
+
+    for c in (c_rstate, c_rlam, c_rdis, *c_pup, *c_pdn, *c_lam, c_dpup, c_dpdn, *r_pup, *r_pdn, r_rad, r_rdis):
         c.wait_send()
 
     @pl.when(jnp.logical_not(first))
@@ -698,13 +728,13 @@
         scratch = [
             vm(8 * ROWS), vm(8 * ROWS), vm(48), vm(8 * ROWS), vm(8 * ROWS), vm(16),
             vm(8 * GROWS), vm(8 * GROWS), vm(8 * GROWS), vm(8 * GROWS), vm(8), vm(8), vm(16), vm(16),
-            vm(8 * GROWS), vm(8 * GROWS), vm(8 * GROWS), vm(8 * GROWS),
+            vm(8 * GROWS), vm(8 * GROWS), vm(8 * GROWS), vm(8 * GROWS), vm(8 * GROWS), vm(8 * GROWS),
             vm(NV, 8, 8, 8), vm(NV, 8, 8, 8), vm(NV, CELLS, 8), vm(NV, CELLS, 8), vm(8 * ROWS),
             vm(24), vm(24), vm(16), vm(16, 8), vm(24, 8), vm(24, 8), vm(16, 8), vm(16, 8),
             vm(8 * GROWS), vm(8 * GROWS), vm(8 * GROWS), vm(8 * GROWS),
             vm(8 * GROWS), vm(8 * GROWS), vm(8 * GROWS), vm(8 * GROWS),
             vm(NV, CELLS, 8), vm(16), vm(16),
-            pltpu.SemaphoreType.DMA((3,)), pltpu.SemaphoreType.DMA((21,)), pltpu.SemaphoreType.DMA((21,)),
+            pltpu.SemaphoreType.DMA((3,)), pltpu.SemaphoreType.DMA((23,)), pltpu.SemaphoreType.DMA((23,)),
         ]
         any_spec = pl.BlockSpec(memory_space=pl.ANY)
         vmem_spec = pl.BlockSpec(memory_space=pltpu.VMEM)

time: 28.7 us -> 27.2 us (0.948)
  Pallas kernels: 25.6 us -> 24 us
    pallas_call x1, Pallas kernels: 25.6 us -> 24 us  [body(): pl.pallas_call(lambda *refs: kernel(sizes, *refs), out_shape=(jax.ShapeDt...]
where the time goes in v2:
time: 27.2 us; the launch traced here: 27 us
  Pallas kernels  24 us (88%)
  local copies, waits for them, and re-layouts  2.35 us (9%)
  between operations  0.65 us (2%)
    pallas_call x1, Pallas kernels, body(): pl.pallas_call(lambda *refs: kernel(sizes, *refs), out_shape=(jax.ShapeDt...  24 us
    unnamed x4, local copies, waits for them, and re-layouts  2.35 us

profile of v2, /device:TPU:0, one launch (start us, length us, event | category | flops | bytes accessed | tf_op | source)
XLA Modules:
  0.0 27.0 jit_solution(18014917504942716827)
XLA Ops:
  0.6 24.0 %adjoint.1 = (f32[672,128]{1,0:T(8,128)}, f32[48,128]{1,0:T(8,128)}) custom-call(f32[672,128]{1,0:T(8,128)} %bitcast.5, f32[672,128]{1,0:T(8,128)} %bitcast.6, f32[48,128]{1,0:T(8,128)} %bitcast.8), custom_call_target="tpu_custom_call" | custom-call | tf_op jit(solution)/shard_map/adjoint/pallas_call | solution.py:741
  24.7 0.0 copy-start
  24.7 1.7 %copy.7 = f32[7,6,4,4,128]{4,3,2,1,0:T(4,128)} copy(f32[7,6,4,4,128]{4,3,2,1,0:T(4,128)} %bitcast.7) | data formatting | bytes 688128
  26.4 0.0 copy-done
  26.4 0.6 %copy.8 = f32[3,4,4,128]{3,2,1,0:T(4,128)} copy(f32[3,4,4,128]{3,2,1,0:T(4,128)S(1)} %bitcast.9) | data formatting | bytes 49152
Async XLA Ops:
  24.7 1.7 %copy-start = (f32[48,128]{1,0:T(8,128)S(1)}, f32[48,128]{1,0:T(8,128)}, u32[]{:S(2)}) copy-start(f32[48,128]{1,0:T(8,128)} %get-tuple-element.5) | copy-start | bytes 73732
